TPU v7x, 512 devices: a whole 4x4x16 slice. The times are simulated.
512 devices in a mesh: tile: 128 (over z, y, core), lvl: 4 (over x).
Axes of the slice: x: 4, y: 4, z: 16, core: 2. Of those that a mesh axis runs over, the one named last changes fastest.
Arguments:
- coefficients: float32 [5, 65536, 512], P(None, 'tile', 'lvl'), may hold values from -0.3 to 2.7, as said below
- level_masks: int32 [512, 4, 6], P('tile', 'lvl'), may hold values 0 or 1
Outputs:
- advanced: float32 [5, 65536, 512], P(None, 'tile', 'lvl')
- tendency: float32 [5, 65536, 512], P(None, 'tile', 'lvl')
Inputs may be any that keep to these rules, and one draw needn't show every extreme that they name: Level-0 coefficients hold the field values there: density in 0.9 to 1.1, each momentum within -0.3 to 0.3, energy in 2.3 to 2.7; every other coefficient lies within -0.006 to 0.006. `level_masks`: 1 keeps that detail level of that tile.
All inputs are finite; a program needn't handle non-finite values. No bound on the sum of `level_masks` on one device may be relied on, other than what follows from the above.
Results may differ from a plain program's by a relative error of at most 0.0003.
Values sent between devices are 32-bit elements; how exact they have to be, the bound alone decides.
A program may use at most 64 MiB of HBM per device.

v0:
```python
import jax
import jax.numpy as jnp
import numpy as np
from jax import lax
from jax.sharding import PartitionSpec as P

LEVELS = 6


gamma_ratio = 1.4
courant = 0.5


def with_halo(cells, sides, width):
    for axis, dim in sides:
        count = lax.axis_size(axis)
        head = lax.slice_in_dim(cells, 0, width, axis=dim)
        tail = lax.slice_in_dim(cells, cells.shape[dim] - width, cells.shape[dim], axis=dim)
        cells = jnp.concatenate(
            [
                lax.ppermute(tail, axis, [(i, (i + 1) % count) for i in range(count)]),
                cells,
                lax.ppermute(head, axis, [((i + 1) % count, i) for i in range(count)]),
            ],
            axis=dim,
        )
    return cells


def level_table(cell_size, levels):
    grades = np.zeros(cell_size, np.int64)
    for position in range(cell_size):
        if position % (cell_size // 2) != 0:
            trailing = (position & -position).bit_length() - 1
            grades[position] = levels - trailing
    return grades


def lift_tables(cell_size, levels):
    grades = level_table(cell_size, levels)
    synthesis = np.eye(cell_size)
    analysis = np.eye(cell_size)
    for level_now in range(1, levels + 1):
        stride = cell_size // 2 ** (level_now + 1)
        for position in range(cell_size):
            if grades[position] == level_now:
                if position + stride < cell_size:
                    synthesis[position] = synthesis[position] + 0.5 * (
                        synthesis[position - stride] + synthesis[position + stride]
                    )
                    analysis[position, position - stride] = -0.5
                    analysis[position, position + stride] = -0.5
                else:
                    synthesis[position] = synthesis[position] + synthesis[position - stride]
                    analysis[position, position - stride] = -1.0
    return (synthesis, analysis)


def level_onehot(cell_size, levels):
    grades = level_table(cell_size, levels)
    joint_grade = np.maximum(grades[:, None], grades[None, :])
    return (joint_grade[None] == np.arange(levels + 1)[:, None, None]).astype(np.float32)


def keep_mask(level_masks, onehot):
    ones_column = jnp.ones(level_masks.shape[:2] + (1,), jnp.float32)
    extended = jnp.concatenate([ones_column, level_masks.astype(jnp.float32)], 2)
    keep_table = jnp.einsum("abl,lij->aibj", extended, onehot)
    return keep_table.reshape(
        level_masks.shape[0] * onehot.shape[1], level_masks.shape[1] * onehot.shape[2]
    )


def transform(field_block, matrix):
    fields, rows_all, columns = field_block.shape
    cell_size = matrix.shape[0]
    blocks = field_block.reshape(
        fields, rows_all // cell_size, cell_size, columns // cell_size, cell_size
    )
    inner_pass = jnp.einsum("ftkbl,jl->ftkbj", blocks, matrix, precision=lax.Precision.HIGHEST)
    outer_pass = jnp.einsum("ik,ftkbj->ftibj", matrix, inner_pass, precision=lax.Precision.HIGHEST)
    return outer_pass.reshape(fields, rows_all, columns)


def primitives(field_state):
    density = field_state[0]
    inverse = 1.0 / density
    velocity_x = field_state[1] * inverse
    velocity_y = field_state[2] * inverse
    velocity_z = field_state[3] * inverse
    kinetic = 0.5 * (
        field_state[1] * velocity_x + field_state[2] * velocity_y + field_state[3] * velocity_z
    )
    pressure = (gamma_ratio - 1.0) * (field_state[4] - kinetic)
    return (density, velocity_x, velocity_y, velocity_z, pressure)


def x_flux_of(field_state):
    density, velocity_x, velocity_y, velocity_z, pressure = primitives(field_state)
    return jnp.stack(
        [
            field_state[1],
            field_state[1] * velocity_x + pressure,
            field_state[2] * velocity_x,
            field_state[3] * velocity_x,
            (field_state[4] + pressure) * velocity_x,
        ]
    )


def y_flux_of(field_state):
    density, velocity_x, velocity_y, velocity_z, pressure = primitives(field_state)
    return jnp.stack(
        [
            field_state[2],
            field_state[1] * velocity_y,
            field_state[2] * velocity_y + pressure,
            field_state[3] * velocity_y,
            (field_state[4] + pressure) * velocity_y,
        ]
    )


def slope_along(padded, direction, spacing):
    if direction == 1:
        return (padded[:, :-4] - 8.0 * padded[:, 1:-3] + 8.0 * padded[:, 3:-1] - padded[:, 4:]) / (
            12.0 * spacing
        )
    return (
        padded[:, :, :-4] - 8.0 * padded[:, :, 1:-3] + 8.0 * padded[:, :, 3:-1] - padded[:, :, 4:]
    ) / (12.0 * spacing)


def signal_speed(field_state):
    density, velocity_x, velocity_y, velocity_z, pressure = primitives(field_state)
    sound = jnp.sqrt(gamma_ratio * pressure / density)
    return jnp.max(jnp.maximum(jnp.abs(velocity_x), jnp.abs(velocity_y)) + sound)


def local_tendency(field_state, spacing):
    padded = with_halo(field_state, (("tile", 1), ("lvl", 2)), 2)
    flux_x = x_flux_of(padded[:, :, 2:-2])
    flux_y = y_flux_of(padded[:, 2:-2, :])
    return -(slope_along(flux_x, 1, spacing) + slope_along(flux_y, 2, spacing))


def shards(coefficients, level_masks):
    cell_size = 2 * 2**LEVELS
    synthesis, analysis = lift_tables(cell_size, LEVELS)
    synthesis = jnp.asarray(synthesis, jnp.float32)
    analysis = jnp.asarray(analysis, jnp.float32)
    onehot = jnp.asarray(level_onehot(cell_size, LEVELS), jnp.float32)
    keep_table = keep_mask(level_masks, onehot)
    spacing = 1.0 / cell_size
    masked_start = coefficients * keep_table
    state_zero = transform(masked_start, synthesis)
    top_speed = lax.pmax(signal_speed(state_zero), ("tile", "lvl"))
    time_step = courant * spacing / top_speed
    rate_zero = keep_table * transform(local_tendency(state_zero, spacing), analysis)
    section_one = masked_start + time_step * rate_zero
    state_one = transform(section_one, synthesis)
    rate_one = keep_table * transform(local_tendency(state_one, spacing), analysis)
    rate_total = 0.5 * (rate_zero + rate_one)
    return (masked_start + time_step * rate_total, rate_total)


def solution(mesh):
    in_specs = (P(None, "tile", "lvl"), P("tile", "lvl", None))
    out_specs = (P(None, "tile", "lvl"), P(None, "tile", "lvl"))
    return jax.shard_map(shards, mesh=mesh, in_specs=in_specs, out_specs=out_specs, check_vma=False)
```

profile of v0, /device:TPU:2, one launch (start us, length us, event | category | flops | bytes accessed | tf_op | source)
XLA Modules:
  0.0 181.9 jit_solution(6050154211258424559)
XLA Ops:
  0.6 0.7 convert_element_type.3
  1.3 0.1 concatenate.15
  1.4 1.2 convolution_bitcast_fusion
  2.6 0.0 copy-start.5
  2.6 1.4 broadcast_multiply_fusion.1
  4.0 1.2 fusion.47
  5.2 1.3 fusion.48
  6.5 0.4 copy.9
  6.9 0.9 fusion.46
  7.9 13.3 %collective-permute-start.1 = (f32[5,2,128]{1,2,0:T(8,128)}, f32[5,2,128]{1,2,0:T(8,128)S(1)}, u32[]{:S(2)}, u32[]{:S(2)}) collective-permute-start(f32[5,2,128]{1,2,0:T(8,128)} %get-tuple-element.33), channel_id=1, source_target_pairs={{4,0},{8,4},{12,8},{16,12},{20,16},{24,20},{28,24},{32,28},{36,32}... | collective-permute-start | bytes 15368 | tf_op jit(solution)/shard_map/ppermute | solution.py:23
  21.2 1.9 %collective-permute-start = (f32[5,2,128]{1,2,0:T(8,128)}, f32[5,2,128]{1,2,0:T(8,128)S(1)}, u32[]{:S(2)}, u32[]{:S(2)}) collective-permute-start(f32[5,2,128]{1,2,0:T(8,128)} %get-tuple-element.32), channel_id=1, source_target_pairs={{0,4},{4,8},{8,12},{12,16},{16,20},{20,24},{24,28},{28,32},{32,36}... | collective-permute-start | bytes 15368 | tf_op jit(solution)/shard_map/ppermute | solution.py:21
  23.1 0.9 fusion.42
  23.9 102.0 %pmax.7 = f32[]{:T(128)} all-reduce(f32[]{:T(128)} %fusion.42), channel_id=1, replica_groups=mesh['tile'=128,'lvl'=4] {'tile','lvl'}, use_global_device_ids=true, to_apply=%region_1.0 | all-reduce | flops 1 | bytes 8 | tf_op jit(solution)/shard_map/pmax | solution.py:157
  126.6 0.1 pad_maximum_fusion.19
  126.7 4.6 %collective-permute-start.3 = (f32[5,516,2]{1,2,0:T(2,128)S(1)}, f32[5,516,2]{1,2,0:T(2,128)S(1)}, u32[]{:S(2)}, u32[]{:S(2)}) collective-permute-start(f32[5,516,2]{1,2,0:T(2,128)S(1)} %get-tuple-element.29), channel_id=1, source_target_pairs={{1,0},{2,1},{3,2},{0,3},{5,4},{6,5},{7,6},{4,7},{9,8},{10,9},{11,1... | collective-permute-start | bytes 61928 | tf_op jit(solution)/shard_map/ppermute | solution.py:23
  131.3 2.1 %collective-permute-start.2 = (f32[5,516,2]{1,2,0:T(2,128)S(1)}, f32[5,516,2]{1,2,0:T(2,128)S(1)}, u32[]{:S(2)}, u32[]{:S(2)}) collective-permute-start(f32[5,516,2]{1,2,0:T(2,128)S(1)} %get-tuple-element.28), channel_id=1, source_target_pairs={{0,1},{1,2},{2,3},{3,0},{4,5},{5,6},{6,7},{7,4},{8,9},{9,10},{10,1... | collective-permute-start | bytes 61928 | tf_op jit(solution)/shard_map/ppermute | solution.py:21
  133.4 0.6 pad_maximum_fusion
  134.0 0.2 add_dynamic-update-slice_fusion.1
  134.2 0.1 multiply_dynamic-update-slice_fusion.5
  134.3 0.1 multiply_dynamic-update-slice_fusion.4
  134.3 0.1 multiply_dynamic-update-slice_fusion.3
  134.4 2.7 %collective-permute-done.2 = f32[5,516,2]{1,2,0:T(2,128)S(1)} collective-permute-done((f32[5,516,2]{1,2,0:T(2,128)S(1)}, f32[5,516,2]{1,2,0:T(2,128)S(1)}, u32[]{:S(2)}, u32[]{:S(2)}) %collective-permute-start.2) | collective-permute-done | bytes 20672 | tf_op jit(solution)/shard_map/ppermute | solution.py:21
  137.1 0.1 constant_dynamic-update-slice_fusion
  137.2 0.1 multiply_dynamic-update-slice_fusion.11
  137.3 0.3 add_dynamic-update-slice_fusion.3
  137.6 0.1 multiply_dynamic-update-slice_fusion.10
  137.6 0.2 multiply_dynamic-update-slice_fusion.9
  137.8 1.1 fusion.9
  138.9 0.0 copy-start.3
  138.9 0.4 copy.19
  139.3 0.4 copy-done.3
  139.7 1.2 fusion.49
  140.9 1.3 fusion.50
  142.2 0.0 copy-done
  142.3 0.2 multiply_add_fusion.1
  142.5 0.8 copy-done.1
  143.3 1.2 fusion.51
  144.5 2.4 %fusion.52 = f32[5,4,128,128]{2,3,1,0:T(8,128)} fusion(f32[5,4,128,128]{3,2,1,0:T(8,128)S(1)} %fusion.51, f32[128,128,1,1]{1,0,3,2:T(8,128)S(1)} %copy-done.6), kind=kOutput, calls=%fused_computation.126 | convolution fusion | flops 503316480 | bytes 2686976 | tf_op jit(solution)/shard_map/ik,ftkbj->ftibj/dot_general | solution.py:81
  146.9 1.7 copy.13
  148.6 0.9 fusion.45
  149.5 1.9 %collective-permute-start.5 = (f32[5,2,128]{1,2,0:T(8,128)}, f32[5,2,128]{1,2,0:T(8,128)S(1)}, u32[]{:S(2)}, u32[]{:S(2)}) collective-permute-start(f32[5,2,128]{1,2,0:T(8,128)} %get-tuple-element.31), channel_id=1, source_target_pairs={{4,0},{8,4},{12,8},{16,12},{20,16},{24,20},{28,24},{32,28},{36,32}... | collective-permute-start | bytes 15368 | tf_op jit(solution)/shard_map/ppermute | solution.py:23
  151.4 2.4 %collective-permute-start.4 = (f32[5,2,128]{1,2,0:T(8,128)}, f32[5,2,128]{1,2,0:T(8,128)S(1)}, u32[]{:S(2)}, u32[]{:S(2)}) collective-permute-start(f32[5,2,128]{1,2,0:T(8,128)} %get-tuple-element.30), channel_id=1, source_target_pairs={{0,4},{4,8},{8,12},{12,16},{16,20},{20,24},{24,28},{28,32},{32,36}... | collective-permute-start | bytes 15368 | tf_op jit(solution)/shard_map/ppermute | solution.py:21
  153.9 2.5 %collective-permute-done.5 = f32[5,2,128]{1,2,0:T(8,128)S(1)} collective-permute-done((f32[5,2,128]{1,2,0:T(8,128)}, f32[5,2,128]{1,2,0:T(8,128)S(1)}, u32[]{:S(2)}, u32[]{:S(2)}) %collective-permute-start.5) | collective-permute-done | bytes 5152 | tf_op jit(solution)/shard_map/ppermute | solution.py:23
  156.3 7.0 %collective-permute-done.4 = f32[5,2,128]{1,2,0:T(8,128)S(1)} collective-permute-done((f32[5,2,128]{1,2,0:T(8,128)}, f32[5,2,128]{1,2,0:T(8,128)S(1)}, u32[]{:S(2)}, u32[]{:S(2)}) %collective-permute-start.4) | collective-permute-done | bytes 5152 | tf_op jit(solution)/shard_map/ppermute | solution.py:21
  163.4 0.1 pad_maximum_fusion.17
  163.5 3.7 %collective-permute-start.7 = (f32[5,516,2]{1,2,0:T(2,128)S(1)}, f32[5,516,2]{1,2,0:T(2,128)S(1)}, u32[]{:S(2)}, u32[]{:S(2)}) collective-permute-start(f32[5,516,2]{1,2,0:T(2,128)S(1)} %get-tuple-element.27), channel_id=1, source_target_pairs={{1,0},{2,1},{3,2},{0,3},{5,4},{6,5},{7,6},{4,7},{9,8},{10,9},{11,1... | collective-permute-start | bytes 61928 | tf_op jit(solution)/shard_map/ppermute | solution.py:23
  167.2 2.4 %collective-permute-start.6 = (f32[5,516,2]{1,2,0:T(2,128)S(1)}, f32[5,516,2]{1,2,0:T(2,128)S(1)}, u32[]{:S(2)}, u32[]{:S(2)}) collective-permute-start(f32[5,516,2]{1,2,0:T(2,128)S(1)} %get-tuple-element.26), channel_id=1, source_target_pairs={{0,1},{1,2},{2,3},{3,0},{4,5},{5,6},{6,7},{7,4},{8,9},{9,10},{10,1... | collective-permute-start | bytes 61928 | tf_op jit(solution)/shard_map/ppermute | solution.py:21
  169.6 0.6 pad_maximum_fusion.1
  170.2 0.2 add_dynamic-update-slice_fusion
  170.3 0.1 multiply_dynamic-update-slice_fusion.2
  170.4 0.1 multiply_dynamic-update-slice_fusion.1
  170.4 0.1 multiply_dynamic-update-slice_fusion
  170.5 2.4 %collective-permute-done.6 = f32[5,516,2]{1,2,0:T(2,128)S(1)} collective-permute-done((f32[5,516,2]{1,2,0:T(2,128)S(1)}, f32[5,516,2]{1,2,0:T(2,128)S(1)}, u32[]{:S(2)}, u32[]{:S(2)}) %collective-permute-start.6) | collective-permute-done | bytes 20672 | tf_op jit(solution)/shard_map/ppermute | solution.py:21
  172.9 0.1 constant_dynamic-update-slice_fusion.1
  173.0 0.1 multiply_dynamic-update-slice_fusion.8
  173.2 0.3 add_dynamic-update-slice_fusion.2
  173.4 0.1 multiply_dynamic-update-slice_fusion.7
  173.5 0.2 multiply_dynamic-update-slice_fusion.6
  173.7 2.1 %fusion.2 = f32[5,512,128]{1,2,0:T(8,128)} fusion(f32[5,512,132]{1,2,0:T(8,128)S(1)} %multiply_dynamic-update-slice_fusion.6, f32[5,516,128]{1,2,0:T(8,128)S(1)} %multiply_dynamic-update-slice_fusion), kind=kLoop, calls=%fused_computation.5 | loop fusion | flops 4259840 | bytes 11796480 | tf_op jit(solution)/shard_map/neg | solution.py:144
  175.8 1.7 copy.20
  177.6 1.2 fusion.53
  178.8 1.3 fusion.54
  180.1 0.0 copy-done.2
  180.1 1.9 %broadcast_multiply_fusion = (f32[5,512,128]{2,1,0:T(8,128)}, f32[5,512,128]{2,1,0:T(8,128)}) fusion(f32[5,4,128,128]{2,3,1,0:T(8,128)S(1)} %fusion.54, f32[5,4,128,128]{2,3,1,0:T(8,128)S(1)} %copy-done.2, f32[512,128]{1,0:T(8,128)S(1)} %bitcast.80, f32[]{:T(128)S(6)} %mul.395, f32[5,512,128]{2,1,0:T(8,128)S(1)} %copy-done), kind=kLoop, calls=%fused_computation.34 | loop fusion | flops 2293760 | bytes 6815748 | tf_op jit(solution)/shard_map/mul | solution.py:163
  (15 shorter events, 0.1 us)
Async XLA Ops:
  2.6 1.5 copy-start.5
  7.9 118.7 %collective-permute-start.1 = (f32[5,2,128]{1,2,0:T(8,128)}, f32[5,2,128]{1,2,0:T(8,128)S(1)}, u32[]{:S(2)}, u32[]{:S(2)}) collective-permute-start(f32[5,2,128]{1,2,0:T(8,128)} %get-tuple-element.33), channel_id=1, source_target_pairs={{4,0},{8,4},{12,8},{16,12},{20,16},{24,20},{28,24},{32,28},{36,32}... | collective-permute-start | bytes 15368 | tf_op jit(solution)/shard_map/ppermute | solution.py:23
  21.2 105.4 %collective-permute-start = (f32[5,2,128]{1,2,0:T(8,128)}, f32[5,2,128]{1,2,0:T(8,128)S(1)}, u32[]{:S(2)}, u32[]{:S(2)}) collective-permute-start(f32[5,2,128]{1,2,0:T(8,128)} %get-tuple-element.32), channel_id=1, source_target_pairs={{0,4},{4,8},{8,12},{12,16},{16,20},{20,24},{24,28},{28,32},{32,36}... | collective-permute-start | bytes 15368 | tf_op jit(solution)/shard_map/ppermute | solution.py:21
  126.7 7.7 %collective-permute-start.3 = (f32[5,516,2]{1,2,0:T(2,128)S(1)}, f32[5,516,2]{1,2,0:T(2,128)S(1)}, u32[]{:S(2)}, u32[]{:S(2)}) collective-permute-start(f32[5,516,2]{1,2,0:T(2,128)S(1)} %get-tuple-element.29), channel_id=1, source_target_pairs={{1,0},{2,1},{3,2},{0,3},{5,4},{6,5},{7,6},{4,7},{9,8},{10,9},{11,1... | collective-permute-start | bytes 61928 | tf_op jit(solution)/shard_map/ppermute | solution.py:23
  131.3 5.7 %collective-permute-start.2 = (f32[5,516,2]{1,2,0:T(2,128)S(1)}, f32[5,516,2]{1,2,0:T(2,128)S(1)}, u32[]{:S(2)}, u32[]{:S(2)}) collective-permute-start(f32[5,516,2]{1,2,0:T(2,128)S(1)} %get-tuple-element.28), channel_id=1, source_target_pairs={{0,1},{1,2},{2,3},{3,0},{4,5},{5,6},{6,7},{7,4},{8,9},{9,10},{10,1... | collective-permute-start | bytes 61928 | tf_op jit(solution)/shard_map/ppermute | solution.py:21
  138.9 0.8 copy-start.3
  140.9 1.3 copy-start
  142.3 1.1 copy-start.1
  142.3 1.0 copy-start.6
  149.5 6.8 %collective-permute-start.5 = (f32[5,2,128]{1,2,0:T(8,128)}, f32[5,2,128]{1,2,0:T(8,128)S(1)}, u32[]{:S(2)}, u32[]{:S(2)}) collective-permute-start(f32[5,2,128]{1,2,0:T(8,128)} %get-tuple-element.31), channel_id=1, source_target_pairs={{4,0},{8,4},{12,8},{16,12},{20,16},{24,20},{28,24},{32,28},{36,32}... | collective-permute-start | bytes 15368 | tf_op jit(solution)/shard_map/ppermute | solution.py:23
  151.4 11.9 %collective-permute-start.4 = (f32[5,2,128]{1,2,0:T(8,128)}, f32[5,2,128]{1,2,0:T(8,128)S(1)}, u32[]{:S(2)}, u32[]{:S(2)}) collective-permute-start(f32[5,2,128]{1,2,0:T(8,128)} %get-tuple-element.30), channel_id=1, source_target_pairs={{0,4},{4,8},{8,12},{12,16},{16,20},{20,24},{24,28},{28,32},{32,36}... | collective-permute-start | bytes 15368 | tf_op jit(solution)/shard_map/ppermute | solution.py:21
  163.5 7.0 %collective-permute-start.7 = (f32[5,516,2]{1,2,0:T(2,128)S(1)}, f32[5,516,2]{1,2,0:T(2,128)S(1)}, u32[]{:S(2)}, u32[]{:S(2)}) collective-permute-start(f32[5,516,2]{1,2,0:T(2,128)S(1)} %get-tuple-element.27), channel_id=1, source_target_pairs={{1,0},{2,1},{3,2},{0,3},{5,4},{6,5},{7,6},{4,7},{9,8},{10,9},{11,1... | collective-permute-start | bytes 61928 | tf_op jit(solution)/shard_map/ppermute | solution.py:23
  167.2 5.7 %collective-permute-start.6 = (f32[5,516,2]{1,2,0:T(2,128)S(1)}, f32[5,516,2]{1,2,0:T(2,128)S(1)}, u32[]{:S(2)}, u32[]{:S(2)}) collective-permute-start(f32[5,516,2]{1,2,0:T(2,128)S(1)} %get-tuple-element.26), channel_id=1, source_target_pairs={{0,1},{1,2},{2,3},{3,0},{4,5},{5,6},{6,7},{7,4},{8,9},{9,10},{10,1... | collective-permute-start | bytes 61928 | tf_op jit(solution)/shard_map/ppermute | solution.py:21
  175.8 1.8 copy-start.4
  178.8 1.3 copy-start.2
where the time goes:
time: 183 us; the launch traced here: 182 us
  blocking collectives  102 us (56%)
  starting transfers between devices  32.2 us (18%)
  waiting for transfers between devices  14.5 us (8%)
  matrix products  12.1 us (7%)
  other arithmetic  11.8 us (6%)
  local copies, waits for them, and re-layouts  7.54 us (4%)
    pmax x1, blocking collectives, shards(): top_speed = lax.pmax(signal_speed(state_zero), ('tile', 'lvl'))  102 us
    ppermute x4, starting transfers between devices, with_halo(): lax.ppermute(head, axis, [((i + 1) % count, i) for i in range(count)])  23.4 us
    ppermute x4, waiting for transfers between devices, with_halo(): lax.ppermute(tail, axis, [(i, (i + 1) % count) for i in range(count)])  12.1 us
    ppermute x4, starting transfers between devices, with_halo(): lax.ppermute(tail, axis, [(i, (i + 1) % count) for i in range(count)])  8.82 us
    dot_general x4, matrix products, transform(): jnp.einsum('ik,ftkbj->ftibj', matrix, inner_pass, precision=lax.Precision...  6.23 us
    dot_general x4, matrix products, transform(): jnp.einsum('ftkbl,jl->ftkbj', blocks, matrix, precision=lax.Precision.HIG...  4.75 us
  transfers between devices with their start and end apart: 8, of which 4 were waited for; matrix products, arithmetic and copies ran while one was open for 2% of the time, Pallas kernels for 0%

commit v1 on v0

v1 whole, which is shorter than its diff:
```python
import functools

import jax
import jax.numpy as jnp
from jax import lax
from jax.experimental import pallas as pl
from jax.experimental.pallas import tpu as pltpu
from jax.sharding import PartitionSpec as P

MESH = pl.DeviceIdType.MESH
F32 = jnp.float32
BF16 = jnp.bfloat16
FIELDS = 5
CELL = 128
SEG = 64
ROWS = 512
BASE_DENSITY = 1.0
BASE_ENERGY = 2.5
SPACING = 1.0 / CELL


def iota(shape, axis):
    return lax.broadcasted_iota(jnp.int32, shape, axis)


def stride_of(position):
    low = jnp.bitwise_and(position, -position)
    return jnp.where(jnp.bitwise_and(position, 63) == 0, 64, low)


def level_of(stride):
    level = jnp.zeros_like(stride)
    for number in range(1, 7):
        level = jnp.where(stride == 64 >> number, number, level)
    return level


def synthesis_t():
    q, p = iota((CELL, CELL), 0), iota((CELL, CELL), 1)
    s = stride_of(q)
    hat = jnp.maximum(1.0 - jnp.abs(p - q).astype(F32) / s.astype(F32), 0.0)
    return jnp.where(jnp.logical_and(q + s == CELL, p >= q), 1.0, hat)


def analysis_t():
    q, p = iota((CELL, CELL), 0), iota((CELL, CELL), 1)
    s = stride_of(p)
    detail = jnp.bitwise_and(p, 63) != 0
    last = p + s == CELL
    left = jnp.where(jnp.logical_and(detail, q == p - s), jnp.where(last, 1.0, 0.5), 0.0)
    right = jnp.where(
        jnp.logical_and(detail, jnp.logical_and(jnp.logical_not(last), q == p + s)), 0.5, 0.0
    )
    return jnp.where(p == q, 1.0, 0.0) - left - right


def slope_matrix(j, i):
    d = j - i
    near = jnp.where(d == 1, 8.0, 0.0) - jnp.where(d == -1, 8.0, 0.0)
    return near + jnp.where(d == -2, 1.0, 0.0) - jnp.where(d == 2, 1.0, 0.0)


def halo_point(slot):
    return jnp.where(slot < 2, slot - 2, slot + 126)


def dot(a, b):
    return lax.dot_general(a, b, (((1,), (0,)), ((), ())), preferred_element_type=F32)


def halves(x):
    high = x.astype(BF16)
    return high, (x - high.astype(F32)).astype(BF16)


def neighbours(nodes, even):
    following = pltpu.roll(nodes[0], 7, 0)
    end = jnp.where(even, following, nodes[-1])[None]
    return end if nodes.shape[0] == 1 else jnp.concatenate([nodes[1:], end], 0)


def row_synthesis(c, even):
    nodes = c[0:1]
    s = SEG // 2
    while s >= 1:
        count = SEG // (2 * s)
        detail = c.reshape(count, 2 * s, 8, CELL)[:, s]
        middle = detail + 0.5 * (nodes + neighbours(nodes, even))
        nodes = jnp.stack([nodes, middle], 1).reshape(2 * count, 8, CELL)
        s //= 2
    return nodes


def row_analysis(u, even):
    pieces = u[0:1]
    s = SEG // 2
    while s >= 1:
        count = SEG // (2 * s)
        both = u.reshape(count, 2, s, 8, CELL)
        left, middle = both[:, 0, 0], both[:, 1, 0]
        detail = middle - 0.5 * (left + neighbours(left, even))
        pieces = jnp.stack([pieces, detail], 1).reshape(2 * count, 8, CELL)
        s //= 2
    return pieces


def row_level(p):
    return 0 if p == 0 else 6 - ((p & -p).bit_length() - 1)


def primitives(q):
    inverse = 1.0 / q[0]
    vx, vy, vz = q[1] * inverse, q[2] * inverse, q[3] * inverse
    xx, yy, zz = q[1] * vx, q[2] * vy, q[3] * vz
    excess = 0.4 * ((q[4] - BASE_ENERGY) - 0.5 * (xx + yy + zz))
    return inverse, vx, vy, xx, yy, excess


def x_flux(q, prim):
    _, vx, _, xx, _, excess = prim
    enthalpy = q[4] + excess + 0.4 * BASE_ENERGY
    return [q[1], xx + excess, q[2] * vx, q[3] * vx, enthalpy * vx]


def y_flux(q, prim):
    _, _, vy, _, yy, excess = prim
    enthalpy = q[4] + excess + 0.4 * BASE_ENERGY
    return [q[2], q[1] * vy, yy + excess, q[3] * vy, enthalpy * vy]


def speed(prim):
    inverse, vx, vy, _, _, excess = prim
    sound = jnp.sqrt(1.4 * (excess + 0.4 * BASE_ENERGY) * inverse)
    return jnp.maximum(jnp.abs(vx), jnp.abs(vy)) + sound


def pack_edges(u, lane):
    def gather(part):
        width = 64
        while part.shape[0] > 1:
            n = part.shape[0] // 2
            chosen = jnp.bitwise_and(lane + 2, width) != 0
            part = jnp.where(chosen, pltpu.roll(part[n:], width, 2), part[:n])
            width //= 2
        return part[0]

    first, second = gather(u[:32]), pltpu.roll(gather(u[32:]), 2, 1)
    upper = jnp.bitwise_and(lane, 3) >= 2
    return jnp.where(upper, first, second), jnp.where(upper, second, first)


CHUNK = 4


def kernel(
    n_tile, n_lvl, inner,
    coef, masks, adv, ten,
    cin, oadv, oten, st, rr, fx, fy, rate0, wmat, hmask, mk,
    row_snd, row_rcv, col_snd, col_rcv, mx_snd, mx_rcv,
    in_sem, out_sem, row_ss, row_rs, col_ss, col_rs, mx_ss, mx_rs,
):
    outer = n_tile // inner
    tile, lvl = lax.axis_index("tile"), lax.axis_index("lvl")
    z, low = tile // inner, tile % inner
    t_right, t_left = lax.rem(tile + 1, n_tile), lax.rem(tile + n_tile - 1, n_tile)
    l_right, l_left = lax.rem(lvl + 1, n_lvl), lax.rem(lvl + n_lvl - 1, n_lvl)

    load = [
        pltpu.make_async_copy(coef.at[f], cin.at[pl.ds(f * ROWS, ROWS)], in_sem.at[f])
        for f in range(FIELDS)
    ]
    for copy in load:
        copy.start()

    groups = [
        [(tile, lax.rem(lvl + k, n_lvl)) for k in range(1, n_lvl)],
        [(z * inner + lax.rem(low + k, inner), lvl) for k in range(1, inner)],
        [(lax.rem(z + k, outer) * inner + low, lvl) for k in range(1, outer)],
    ]
    barrier = pltpu.get_barrier_semaphore()
    partners = [(t_right, lvl), (t_left, lvl), (tile, l_right), (tile, l_left)]
    partners += groups[0] + groups[1] + groups[2]
    for partner in partners:
        pl.semaphore_signal(barrier, inc=1, device_id=partner, device_id_type=MESH)

    sub, lane = iota((8, CELL), 0), iota((8, CELL), 1)
    even = jnp.bitwise_and(sub, 1) == 0

    synth = synthesis_t().astype(BF16)
    at = analysis_t().astype(BF16)
    k, i = iota((CELL, CELL), 0), iota((CELL, CELL), 1)
    wmat[0, :CELL], wmat[0, CELL:] = synth, synth
    wmat[1, :CELL] = at
    wmat[1, CELL:] = dot(slope_matrix(k, i).astype(BF16), at).astype(BF16)
    for part, offset in ((2, 2), (3, 0)):
        edge = slope_matrix(halo_point(jnp.bitwise_and(k + offset, 3)), i).astype(BF16)
        edge = dot(edge, at).astype(BF16)
        wmat[part, :CELL], wmat[part, CELL:] = edge, edge
    row, col = iota((32 * 8, CELL), 0), iota((32 * 8, CELL), 1)
    for part, offset in ((0, 2), (1, 0)):
        group = jnp.right_shift(jnp.bitwise_and(col + offset, 127), 2)
        hmask[part] = jnp.where(group == jnp.right_shift(row, 3), 1.0, 0.0).astype(BF16)

    level = level_of(stride_of(lane))
    owner = jnp.right_shift(sub, 1)
    planes = [jnp.ones((8, CELL), F32)]
    for number in range(6):
        plane = jnp.full((8, CELL), masks[0, 0, number], jnp.int32)
        for t in range(1, 4):
            plane = jnp.where(owner == t, masks[t, 0, number], plane)
        planes.append(plane.astype(F32))
    for number in range(7):
        keep = planes[number]
        for other in range(number + 1, 7):
            keep = jnp.where(level == other, planes[other], keep)
        mk[number] = keep

    def by_level(scale=None):
        keeps = [mk[number] if scale is None else mk[number] * scale for number in range(7)]
        return lambda p: keeps[row_level(p)]

    def start_of(f, keep_at):
        return [
            cin[pl.ds(f * ROWS + p, 8, SEG), :] * keep_at(p) for p in range(SEG)
        ]

    def base_of(f):
        return jnp.where(f == 0, BASE_DENSITY, jnp.where(f == 4, BASE_ENERGY, 0.0)).astype(F32)

    def synthesise(c):
        high, low_part = halves(c.reshape(ROWS, CELL))
        out = dot(jnp.concatenate([high, low_part], 1), wmat[0])
        return row_synthesis(out.reshape(SEG, 8, CELL), even)

    def send_edges(stage, f, u):
        to_right, to_left = pack_edges(u, lane)
        col_snd[stage, 0, f] = to_right
        col_snd[stage, 1, f] = to_left
        for r in range(2):
            row_snd[stage, 0, pl.ds(2 * f + r, 1), :] = u[62 + r, 7:8]
            row_snd[stage, 1, pl.ds(2 * f + r, 1), :] = u[r, 0:1]

    def edge_copies(stage):
        copies = []
        for side, (t_to, l_to) in enumerate(((t_right, l_right), (t_left, l_left))):
            copies.append(pltpu.make_async_remote_copy(
                col_snd.at[stage, side], col_rcv.at[stage, side],
                col_ss.at[stage, side], col_rs.at[stage, side],
                device_id=(tile, l_to), device_id_type=MESH))
            copies.append(pltpu.make_async_remote_copy(
                row_snd.at[stage, side], row_rcv.at[stage, side],
                row_ss.at[stage, side], row_rs.at[stage, side],
                device_id=(t_to, lvl), device_id_type=MESH))
        return copies

    for copy in load:
        copy.wait()

    def first(f, _):
        base = base_of(f)
        parts = start_of(f, by_level())
        parts[0] = parts[0] - jnp.where(jnp.bitwise_and(lane, 63) == 0, base, 0.0)
        u = synthesise(jnp.stack(parts, 0)) + base
        st[f] = u
        send_edges(0, f, u)
        return 0

    lax.fori_loop(0, FIELDS, first, 0)
    pl.semaphore_wait(barrier, len(partners))
    edges = [edge_copies(0), edge_copies(1)]
    for copy in edges[0]:
        copy.start()

    def fluxes(stage, dt):
        def chunk(c, top):
            at_rows = pl.ds(c * CHUNK, CHUNK)
            q = [st[f, at_rows] for f in range(FIELDS)]
            if stage:
                q = [q[f] + dt * rr[f, at_rows] for f in range(FIELDS)]
            prim = primitives(q)
            for f, value in enumerate(x_flux(q, prim)):
                fx[f, pl.ds(c * CHUNK + 2, CHUNK)] = value
            for f, value in enumerate(y_flux(q, prim)):
                fy[f, at_rows] = value
            if stage == 0:
                top = jnp.maximum(top, jnp.max(speed(prim), 0))
            return top

        return lax.fori_loop(0, SEG // CHUNK, chunk, jnp.zeros((8, CELL), F32))

    def rounds(number):
        copies = []
        for slot, partner in enumerate(groups[number]):
            copies.append(pltpu.make_async_remote_copy(
                mx_snd.at[number], mx_rcv.at[number, slot],
                mx_ss.at[number], mx_rs.at[number],
                device_id=partner, device_id_type=MESH))
        return copies

    def send_top(number, top):
        mx_snd[number] = top
        for copy in rounds(number):
            copy.start()

    def take_top(number, top):
        count = len(groups[number])
        whole = mx_rcv.at[number, pl.ds(0, count)]
        pltpu.make_async_copy(whole, whole, mx_rs.at[number]).wait()
        return jnp.maximum(top, jnp.max(mx_rcv[number, 0:count], 0))

    def ext_rows(stage, f, side, r, dt):
        source = st[f, 62 + r] if side == 0 else st[f, r]
        beyond = row_rcv[0, side, pl.ds(2 * f + r, 1), :]
        if stage:
            source = source + dt * (rr[f, 62 + r] if side == 0 else rr[f, r])
            beyond = beyond + dt[0:1] * row_rcv[1, side, pl.ds(2 * f + r, 1), :]
        rolled = pltpu.roll(source, 1 if side == 0 else 7, 0)
        return jnp.where(sub == (0 if side == 0 else 7), beyond, rolled)

    upper = jnp.bitwise_and(lane, 3) >= 2

    def halo_fluxes(stage, dt):
        q = [
            jnp.stack([ext_rows(stage, f, side, r, dt) for side in range(2) for r in range(2)], 0)
            for f in range(FIELDS)
        ]
        for f, value in enumerate(x_flux(q, primitives(q))):
            fx[f, 0:2] = value[0:2]
            fx[f, SEG + 2:SEG + 4] = value[2:4]
        q = []
        for f in range(FIELDS):
            from_left, from_right = col_rcv[0, 0, f], col_rcv[0, 1, f]
            if stage:
                from_left = from_left + dt * col_rcv[1, 0, f]
                from_right = from_right + dt * col_rcv[1, 1, f]
            q.append(jnp.stack([
                jnp.where(upper, from_left, from_right), jnp.where(upper, from_right, from_left)
            ], 0))
        return y_flux(q, primitives(q))

    def analysed(f, edge):
        g = fx[f]
        slope = 8.0 * (g[3:67] - g[1:65]) - (g[4:68] - g[0:64])
        xh, xl = halves(slope.reshape(ROWS, CELL))
        yh, yl = halves(fy[f].reshape(ROWS, CELL))
        weights = wmat[1]
        out = dot(jnp.concatenate([xh, yh], 1), weights) + dot(jnp.concatenate([xl, yl], 1), weights)
        extra = []
        for part in range(2):
            eh, el = halves(jnp.concatenate([edge[part], edge[part]], 0))
            spread = hmask[part]
            eh = jnp.concatenate([eh] * 16, 0) * spread
            el = jnp.concatenate([el] * 16, 0) * spread
            extra.append(dot(jnp.concatenate([eh, el], 1), wmat[2 + part]))
        out = out + jnp.concatenate(extra, 0)
        return row_analysis(out.reshape(SEG, 8, CELL), even)

    zero = jnp.zeros((8, CELL), F32)
    top = jnp.max(fluxes(0, zero), 0, keepdims=True)
    send_top(0, top)
    for copy in edges[0]:
        copy.wait_recv()
    top = take_top(0, top)
    send_top(1, top)
    edge_flux = halo_fluxes(0, zero)
    scale = -1.0 / (12.0 * SPACING)
    for f in range(FIELDS):
        keep_at = by_level(scale)
        d = analysed(f, edge_flux[f])
        rate = jnp.stack([d[p] * keep_at(p) for p in range(SEG)], 0)
        rate0[f] = rate
        u = synthesise(rate)
        rr[f] = u
        send_edges(1, f, u)
        if f == 2:
            top = take_top(1, top)
            send_top(2, top)
    for copy in edges[1]:
        copy.start()
    top = take_top(2, top)
    top = jnp.max(top, 1, keepdims=True)
    dt = 0.5 * SPACING / jnp.broadcast_to(top, (8, CELL))
    fluxes(1, dt)
    for copy in edges[1]:
        copy.wait_recv()
    edge_flux = halo_fluxes(1, dt)
    store = []
    for f in range(FIELDS):
        keep_at = by_level(0.5 * scale)
        d = analysed(f, edge_flux[f])
        for p in range(SEG):
            value = 0.5 * rate0[f, p] + d[p] * keep_at(p)
            rows = pl.ds(f * ROWS + p, 8, SEG)
            start = cin[rows, :] * mk[row_level(p)]
            oten[rows, :] = value
            oadv[rows, :] = start + dt * value
        for number, (source, target) in enumerate(((oadv, adv), (oten, ten))):
            copy = pltpu.make_async_copy(
                source.at[pl.ds(f * ROWS, ROWS)], target.at[f], out_sem.at[number, f])
            copy.start()
            store.append(copy)
    for copy in edges[0] + edges[1]:
        copy.wait_send()
    for number in range(3):
        for copy in rounds(number):
            copy.wait_send()
    for copy in store:
        copy.wait()


def solution(mesh):
    n_tile, n_lvl = mesh.shape["tile"], mesh.shape["lvl"]
    inner = 8 if n_tile > 8 and n_tile % 8 == 0 else 2
    most = max(n_lvl, inner, n_tile // inner) - 1
    block = (FIELDS, SEG, 8, CELL)
    flat = (FIELDS * ROWS, CELL)
    dma = pltpu.SemaphoreType.DMA

    def shards(coefficients, level_masks):
        result = jax.ShapeDtypeStruct((FIELDS, ROWS, CELL), F32)
        return pl.pallas_call(
            functools.partial(kernel, n_tile, n_lvl, inner),
            out_shape=(result, result),
            in_specs=[
                pl.BlockSpec(memory_space=pl.ANY),
                pl.BlockSpec(memory_space=pltpu.SMEM),
            ],
            out_specs=(pl.BlockSpec(memory_space=pl.ANY), pl.BlockSpec(memory_space=pl.ANY)),
            scratch_shapes=[
                pltpu.VMEM(flat, F32), pltpu.VMEM(flat, F32), pltpu.VMEM(flat, F32),
                pltpu.VMEM(block, F32), pltpu.VMEM(block, F32),
                pltpu.VMEM((FIELDS, SEG + 4, 8, CELL), F32), pltpu.VMEM(block, F32),
                pltpu.VMEM(block, F32),
                pltpu.VMEM((4, 2 * CELL, CELL), BF16), pltpu.VMEM((2, 256, CELL), BF16),
                pltpu.VMEM((7, 8, CELL), F32),
                pltpu.VMEM((2, 2, 16, CELL), F32), pltpu.VMEM((2, 2, 16, CELL), F32),
                pltpu.VMEM((2, 2, FIELDS, 8, CELL), F32), pltpu.VMEM((2, 2, FIELDS, 8, CELL), F32),
                pltpu.VMEM((3, 1, CELL), F32), pltpu.VMEM((3, most, 1, CELL), F32),
                dma((FIELDS,)), dma((2, FIELDS)),
                dma((2, 2)), dma((2, 2)), dma((2, 2)), dma((2, 2)), dma((3,)), dma((3,)),
            ],
            compiler_params=pltpu.CompilerParams(
                collective_id=0, has_side_effects=True, vmem_limit_bytes=40 * 2**20
            ),
        )(coefficients, level_masks)

    specs = P(None, "tile", "lvl")
    return jax.shard_map(
        shards, mesh=mesh, in_specs=(specs, P("tile", "lvl", None)), out_specs=(specs, specs),
        check_vma=False,
    )
```

time: 183 us -> 40.8 us (0.22)
  the two profiles are of different devices: /device:TPU:2 before, /device:TPU:1 now
where the time goes in v1:
time: 40.8 us; the launch traced here: 40.6 us
  Pallas kernels  35.8 us (88%)
  local copies, waits for them, and re-layouts  4.11 us (10%)
  between operations  0.65 us (2%)
    pallas_call x1, Pallas kernels, shards(): pl.pallas_call(functools.partial(kernel, n_tile, n_lvl, inner), out_shape...  35.8 us
    unnamed x6, local copies, waits for them, and re-layouts  4.11 us

profile of v1, /device:TPU:1, one launch (start us, length us, event | category | flops | bytes accessed | tf_op | source)
XLA Modules:
  0.0 40.6 jit_solution(4698974950672852242)
XLA Ops:
  0.6 0.0 copy-start
  0.6 1.3 %copy-done = f32[5,512,128]{2,1,0:T(8,128)S(1)} copy-done((f32[5,512,128]{2,1,0:T(8,128)S(1)}, f32[5,512,128]{2,1,0:T(8,128)}, u32[]{:S(2)}) %copy-start) | copy-done | bytes 1310744
  1.9 0.0 copy-start.1
  1.9 0.7 %copy-done.1 = s32[4,1,6]{2,1,0:T(1,128)S(1)} copy-done((s32[4,1,6]{2,1,0:T(1,128)S(1)}, s32[4,1,6]{2,1,0:T(1,128)}, u32[]{:S(2)}) %copy-start.1) | copy-done | bytes 120
  2.6 35.8 %shard_map.41 = (f32[5,512,128]{2,1,0:T(8,128)S(1)}, f32[5,512,128]{2,1,0:T(8,128)S(1)}) custom-call(f32[5,512,128]{2,1,0:T(8,128)S(1)} %copy-done, s32[4,1,6]{2,1,0:T(1,128)S(1)} %copy-done.1), custom_call_target="tpu_custom_call" | custom-call | tf_op jit(solution)/shard_map/pallas_call | solution.py:421
  38.5 1.1 %copy.6 = f32[5,512,128]{2,1,0:T(8,128)} copy(f32[5,512,128]{2,1,0:T(8,128)S(1)} %get-tuple-element.4) | data formatting | bytes 2621440
  39.5 1.1 %copy.7 = f32[5,512,128]{2,1,0:T(8,128)} copy(f32[5,512,128]{2,1,0:T(8,128)S(1)} %get-tuple-element.5) | data formatting | bytes 2621440
Async XLA Ops:
  0.6 1.3 %copy-start = (f32[5,512,128]{2,1,0:T(8,128)S(1)}, f32[5,512,128]{2,1,0:T(8,128)}, u32[]{:S(2)}) copy-start(f32[5,512,128]{2,1,0:T(8,128)} %coef.1) | copy-start | bytes 3932164
  1.9 0.7 %copy-start.1 = (s32[4,1,6]{2,1,0:T(1,128)S(1)}, s32[4,1,6]{2,1,0:T(1,128)}, u32[]{:S(2)}) copy-start(s32[4,1,6]{2,1,0:T(1,128)} %masks.1) | copy-start | bytes 292

commit v2 on v1

v2 whole, which is shorter than its diff:
```python
import functools

import jax
import jax.numpy as jnp
from jax import lax
from jax.experimental import pallas as pl
from jax.experimental.pallas import tpu as pltpu
from jax.sharding import PartitionSpec as P

MESH = pl.DeviceIdType.MESH
F32 = jnp.float32
BF16 = jnp.bfloat16
FIELDS = 5
CELL = 128
SEG = 64
ROWS = 512
BASE_DENSITY = 1.0
BASE_ENERGY = 2.5
SPACING = 1.0 / CELL


def iota(shape, axis):
    return lax.broadcasted_iota(jnp.int32, shape, axis)


def stride_of(position):
    low = jnp.bitwise_and(position, -position)
    return jnp.where(jnp.bitwise_and(position, 63) == 0, 64, low)


def level_of(stride):
    level = jnp.zeros_like(stride)
    for number in range(1, 7):
        level = jnp.where(stride == 64 >> number, number, level)
    return level


def synthesis_t():
    q, p = iota((CELL, CELL), 0), iota((CELL, CELL), 1)
    s = stride_of(q)
    hat = jnp.maximum(1.0 - jnp.abs(p - q).astype(F32) / s.astype(F32), 0.0)
    return jnp.where(jnp.logical_and(q + s == CELL, p >= q), 1.0, hat)


def analysis_t():
    q, p = iota((CELL, CELL), 0), iota((CELL, CELL), 1)
    s = stride_of(p)
    detail = jnp.bitwise_and(p, 63) != 0
    last = p + s == CELL
    left = jnp.where(jnp.logical_and(detail, q == p - s), jnp.where(last, 1.0, 0.5), 0.0)
    right = jnp.where(
        jnp.logical_and(detail, jnp.logical_and(jnp.logical_not(last), q == p + s)), 0.5, 0.0
    )
    return jnp.where(p == q, 1.0, 0.0) - left - right


def slope_matrix(j, i):
    d = j - i
    near = jnp.where(d == 1, 8.0, 0.0) - jnp.where(d == -1, 8.0, 0.0)
    return near + jnp.where(d == -2, 1.0, 0.0) - jnp.where(d == 2, 1.0, 0.0)


def halo_point(slot):
    return jnp.where(slot < 2, slot - 2, slot + 126)


def dot(a, b):
    return lax.dot_general(a, b, (((1,), (0,)), ((), ())), preferred_element_type=F32)


def halves(x):
    high = x.astype(BF16)
    return high, (x - high.astype(F32)).astype(BF16)


def neighbours(nodes, even):
    following = pltpu.roll(nodes[0], 7, 0)
    end = jnp.where(even, following, nodes[-1])[None]
    return end if nodes.shape[0] == 1 else jnp.concatenate([nodes[1:], end], 0)


def row_synthesis(c, even):
    nodes = c[0:1]
    s = SEG // 2
    while s >= 1:
        count = SEG // (2 * s)
        detail = c.reshape(count, 2 * s, 8, CELL)[:, s]
        middle = detail + 0.5 * (nodes + neighbours(nodes, even))
        nodes = jnp.stack([nodes, middle], 1).reshape(2 * count, 8, CELL)
        s //= 2
    return nodes


def row_analysis(u, even):
    pieces = u[0:1]
    s = SEG // 2
    while s >= 1:
        count = SEG // (2 * s)
        both = u.reshape(count, 2, s, 8, CELL)
        left, middle = both[:, 0, 0], both[:, 1, 0]
        detail = middle - 0.5 * (left + neighbours(left, even))
        pieces = jnp.stack([pieces, detail], 1).reshape(2 * count, 8, CELL)
        s //= 2
    return pieces


def row_level(p):
    return 0 if p == 0 else 6 - ((p & -p).bit_length() - 1)


def primitives(q):
    inverse = 1.0 / q[0]
    vx, vy, vz = q[1] * inverse, q[2] * inverse, q[3] * inverse
    xx, yy, zz = q[1] * vx, q[2] * vy, q[3] * vz
    excess = 0.4 * ((q[4] - BASE_ENERGY) - 0.5 * (xx + yy + zz))
    return inverse, vx, vy, xx, yy, excess


def x_flux(q, prim):
    _, vx, _, xx, _, excess = prim
    enthalpy = q[4] + excess + 0.4 * BASE_ENERGY
    return [q[1], xx + excess, q[2] * vx, q[3] * vx, enthalpy * vx]


def y_flux(q, prim):
    _, _, vy, _, yy, excess = prim
    enthalpy = q[4] + excess + 0.4 * BASE_ENERGY
    return [q[2], q[1] * vy, yy + excess, q[3] * vy, enthalpy * vy]


def speed(prim):
    inverse, vx, vy, _, _, excess = prim
    sound = jnp.sqrt(1.4 * (excess + 0.4 * BASE_ENERGY) * inverse)
    return jnp.maximum(jnp.abs(vx), jnp.abs(vy)) + sound


def pack_edges(u, lane):
    def gather(part):
        width = 64
        while part.shape[0] > 1:
            n = part.shape[0] // 2
            chosen = jnp.bitwise_and(lane + 2, width) != 0
            part = jnp.where(chosen, pltpu.roll(part[n:], width, 2), part[:n])
            width //= 2
        return part[0]

    first, second = gather(u[:32]), pltpu.roll(gather(u[32:]), 2, 1)
    upper = jnp.bitwise_and(lane, 3) >= 2
    return jnp.where(upper, first, second), jnp.where(upper, second, first)


CHUNK = 4
EXT = SEG + 4


def flux_pass(state_at, fx, fy):
    def chunk(c, _):
        rows = pl.ds(c * CHUNK, CHUNK)
        q = state_at(rows)
        prim = primitives(q)
        for f, value in enumerate(x_flux(q, prim)):
            fx[f, rows] = value
        for f, value in enumerate(y_flux(q, prim)):
            fy[f, rows] = value
        return 0

    lax.fori_loop(0, EXT // CHUNK, chunk, 0)


def analysed(f, edge, fx, fy, wmat, hmask, even):
    g = fx[f]
    slope = 8.0 * (g[3:67] - g[1:65]) - (g[4:68] - g[0:64])
    xh, xl = halves(slope.reshape(ROWS, CELL))
    yh, yl = halves(fy[f, 2:66].reshape(ROWS, CELL))
    weights = wmat[1]
    out = dot(jnp.concatenate([xh, yh], 1), weights) + dot(jnp.concatenate([xl, yl], 1), weights)
    extra = []
    for part in range(2):
        eh, el = halves(jnp.concatenate([edge[part], edge[part]], 0))
        spread = hmask[part]
        eh = jnp.concatenate([eh] * 16, 0) * spread
        el = jnp.concatenate([el] * 16, 0) * spread
        extra.append(dot(jnp.concatenate([eh, el], 1), wmat[2 + part]))
    out = out + jnp.concatenate(extra, 0)
    return row_analysis(out.reshape(SEG, 8, CELL), even)


def build_weights(wmat, hmask):
    synth = synthesis_t().astype(BF16)
    at = analysis_t().astype(BF16)
    k, i = iota((CELL, CELL), 0), iota((CELL, CELL), 1)
    wmat[0, :CELL], wmat[0, CELL:] = synth, synth
    wmat[1, :CELL] = at
    wmat[1, CELL:] = dot(slope_matrix(k, i).astype(BF16), at).astype(BF16)
    for part, offset in ((2, 2), (3, 0)):
        edge = slope_matrix(halo_point(jnp.bitwise_and(k + offset, 3)), i).astype(BF16)
        edge = dot(edge, at).astype(BF16)
        wmat[part, :CELL], wmat[part, CELL:] = edge, edge
    row, col = iota((32 * 8, CELL), 0), iota((32 * 8, CELL), 1)
    for part, offset in ((0, 2), (1, 0)):
        group = jnp.right_shift(jnp.bitwise_and(col + offset, 127), 2)
        hmask[part] = jnp.where(group == jnp.right_shift(row, 3), 1.0, 0.0).astype(BF16)


def build_keep(masks, mk, mkd, sub, lane):
    level = level_of(stride_of(lane))
    owner = jnp.right_shift(sub, 1)
    planes = [jnp.ones((8, CELL), F32)]
    for number in range(6):
        plane = jnp.full((8, CELL), masks[0, 0, number], jnp.int32)
        for t in range(1, 4):
            plane = jnp.where(owner == t, masks[t, 0, number], plane)
        planes.append(plane.astype(F32))
    for number in range(7):
        keep = planes[number]
        for other in range(number + 1, 7):
            keep = jnp.where(level == other, planes[other], keep)
        mk[number] = keep
        mkd[number] = keep * (-0.5 / (12.0 * SPACING))


def front(
    n_tile, n_lvl, inner, reach,
    coef, masks,
    start, half0, st, rr, cols, dts, wmat, hmask, mkd,
    cin, lvm, fx, fy, mk,
    row_snd, row_rcv, col_snd, col_rcv, mx_snd, mx_rcv,
    in_sem, mask_sem, row_ss, row_rs, col_ss, col_rs, mx_ss, mx_rs,
):
    outer = n_tile // inner
    tile, lvl = lax.axis_index("tile"), lax.axis_index("lvl")
    z, low = tile // inner, tile % inner
    t_right, t_left = lax.rem(tile + 1, n_tile), lax.rem(tile + n_tile - 1, n_tile)
    l_right, l_left = lax.rem(lvl + 1, n_lvl), lax.rem(lvl + n_lvl - 1, n_lvl)

    load_masks = pltpu.make_async_copy(masks, lvm, mask_sem)
    load_masks.start()
    load = [
        pltpu.make_async_copy(coef.at[f], cin.at[pl.ds(f * ROWS, ROWS)], in_sem.at[f])
        for f in range(FIELDS)
    ]
    for copy in load:
        copy.start()

    def there(dz, dlow, dx):
        to = lax.rem(z + outer + dz, outer) * inner + lax.rem(low + dlow, inner)
        return to, lax.rem(lvl + dx, n_lvl)

    spread = sorted(range(-reach, reach + 1), key=lambda d: -abs(d))
    jumps = sorted({d % outer for d in (-reach, 0, reach)}, key=lambda d: d == 0)
    spread = list(dict.fromkeys(d % outer for d in spread))
    groups = [
        [there(dz, 0, dx) for dz in spread for dx in range(n_lvl) if dz or dx],
        [there(dz, dlow, 0) for dz in jumps for dlow in range(inner) if dz or dlow],
    ]
    partners = groups[0] + groups[1]
    partners += [(t_right, lvl), (t_left, lvl), (tile, l_right), (tile, l_left)]
    barrier = pltpu.get_barrier_semaphore()
    for partner in partners:
        pl.semaphore_signal(barrier, inc=1, device_id=partner, device_id_type=MESH)

    sub, lane = iota((8, CELL), 0), iota((8, CELL), 1)
    even = jnp.bitwise_and(sub, 1) == 0
    upper = jnp.bitwise_and(lane, 3) >= 2
    coarse = jnp.bitwise_and(lane, 63) == 0
    build_weights(wmat, hmask)
    load_masks.wait()
    build_keep(lvm, mk, mkd, sub, lane)

    def synthesise(c):
        high, low_part = halves(c.reshape(ROWS, CELL))
        out = dot(jnp.concatenate([high, low_part], 1), wmat[0])
        return row_synthesis(out.reshape(SEG, 8, CELL), even)

    def pack(stage, f, u):
        to_right, to_left = pack_edges(u, lane)
        col_snd[stage, 0, f] = to_right
        col_snd[stage, 1, f] = to_left
        for r in range(2):
            row_snd[stage, 0, pl.ds(2 * f + r, 1), :] = u[62 + r, 7:8]
            row_snd[stage, 1, pl.ds(2 * f + r, 1), :] = u[r, 0:1]

    def edge_copies(stage):
        copies = []
        for side, (t_to, l_to) in enumerate(((t_right, l_right), (t_left, l_left))):
            copies.append(pltpu.make_async_remote_copy(
                col_snd.at[stage, side], col_rcv.at[stage, side],
                col_ss.at[stage, side], col_rs.at[stage, side],
                device_id=(tile, l_to), device_id_type=MESH))
            copies.append(pltpu.make_async_remote_copy(
                row_snd.at[stage, side], row_rcv.at[stage, side],
                row_ss.at[stage, side], row_rs.at[stage, side],
                device_id=(t_to, lvl), device_id_type=MESH))
        return copies

    def rounds(number):
        return [
            pltpu.make_async_remote_copy(
                mx_snd.at[number], mx_rcv.at[number, slot], mx_ss.at[number], mx_rs.at[number],
                device_id=partner, device_id_type=MESH)
            for slot, partner in enumerate(groups[number])
        ]

    def take_top(number, top):
        count = len(groups[number])
        whole = mx_rcv.at[number, pl.ds(0, count)]
        pltpu.make_async_copy(whole, whole, mx_rs.at[number]).wait()
        return jnp.maximum(top, jnp.max(mx_rcv[number, 0:count], 0))

    def take_edges(stage, block):
        for f in range(FIELDS):
            for side in range(2):
                for r in range(2):
                    source = block[f, 64 + r] if side == 0 else block[f, 2 + r]
                    beyond = row_rcv[stage, side, pl.ds(2 * f + r, 1), :]
                    rolled = pltpu.roll(source, 1 if side == 0 else 7, 0)
                    here = r if side == 0 else 66 + r
                    block[f, here] = jnp.where(sub == (0 if side == 0 else 7), beyond, rolled)
            from_left, from_right = col_rcv[stage, 0, f], col_rcv[stage, 1, f]
            cols[stage, f, 0] = jnp.where(upper, from_left, from_right)
            cols[stage, f, 1] = jnp.where(upper, from_right, from_left)

    for f in range(FIELDS):
        load[f].wait()
        parts = [cin[pl.ds(f * ROWS + p, 8, SEG), :] * mk[row_level(p)] for p in range(SEG)]
        parts = jnp.stack(parts, 0)
        start[f] = parts
        base = {0: BASE_DENSITY, 4: BASE_ENERGY}.get(f)
        if base:
            first = jnp.where(coarse, parts[0:1] - base, parts[0:1])
            parts = jnp.concatenate([first, parts[1:]], 0)
        u = synthesise(parts)
        if base:
            u = u + base
        st[f, 2:66] = u
        pack(0, f, u)

    def fastest(c, top):
        rows = pl.ds(c * CHUNK + 2, CHUNK)
        prim = primitives([st[f, rows] for f in range(FIELDS)])
        return jnp.maximum(top, jnp.max(speed(prim), 0))

    top = lax.fori_loop(0, SEG // CHUNK, fastest, jnp.zeros((8, CELL), F32))
    top = jnp.max(top, 0, keepdims=True)
    mx_snd[0] = top
    pl.semaphore_wait(barrier, len(partners))
    first_round, second_round = rounds(0), rounds(1)
    edges = [edge_copies(0), edge_copies(1)]
    for copy in first_round + edges[0]:
        copy.start()

    for copy in edges[0]:
        copy.wait_recv()
    take_edges(0, st)
    flux_pass(lambda rows: [st[f, rows] for f in range(FIELDS)], fx, fy)
    q = [cols[0, f] for f in range(FIELDS)]
    edge_flux = y_flux(q, primitives(q))
    for f in range(FIELDS):
        d = analysed(f, edge_flux[f], fx, fy, wmat, hmask, even)
        half = jnp.stack([d[p] * mkd[row_level(p)] for p in range(SEG)], 0)
        half0[f] = half
        u = synthesise(half + half)
        rr[f, 2:66] = u
        pack(1, f, u)
    for copy in edges[1]:
        copy.start()
    top = take_top(0, top)
    mx_snd[1] = top
    for copy in second_round:
        copy.start()
    for copy in edges[1]:
        copy.wait_recv()
    take_edges(1, rr)
    for copy in edges[0] + edges[1] + first_round:
        copy.wait_send()
    top = take_top(1, top)
    top = jnp.max(top, 1, keepdims=True)
    dts[...] = 0.5 * SPACING / jnp.broadcast_to(top, (8, CELL))
    for copy in second_round:
        copy.wait_send()


def back(
    start, half0, st, rr, cols, dts, wmat, hmask, mkd, adv, ten, oadv, oten, fx, fy, out_sem
):
    even = jnp.bitwise_and(iota((8, CELL), 0), 1) == 0
    dt = dts[...]
    flux_pass(lambda rows: [st[f, rows] + dt * rr[f, rows] for f in range(FIELDS)], fx, fy)
    q = [cols[0, f] + dt * cols[1, f] for f in range(FIELDS)]
    edge_flux = y_flux(q, primitives(q))
    store = []
    for f in range(FIELDS):
        d = analysed(f, edge_flux[f], fx, fy, wmat, hmask, even)
        for p in range(SEG):
            value = half0[f, p] + d[p] * mkd[row_level(p)]
            rows = pl.ds(f * ROWS + p, 8, SEG)
            oten[rows, :] = value
            oadv[rows, :] = start[f, p] + dt * value
        for number, (source, target) in enumerate(((oadv, adv), (oten, ten))):
            copy = pltpu.make_async_copy(
                source.at[pl.ds(f * ROWS, ROWS)], target.at[f], out_sem.at[number, f])
            copy.start()
            store.append(copy)
    for copy in store:
        copy.wait()


def solution(mesh):
    n_tile, n_lvl = mesh.shape["tile"], mesh.shape["lvl"]
    inner = 8 if n_tile > 8 and n_tile % 8 == 0 else 2
    reach = -(-(n_tile // inner) // 4)
    block, wide = (FIELDS, SEG, 8, CELL), (FIELDS, EXT, 8, CELL)
    flat = (FIELDS * ROWS, CELL)
    most = max((2 * reach + 1) * n_lvl, 3 * inner)
    dma = pltpu.SemaphoreType.DMA
    between = [
        (block, F32), (block, F32), (wide, F32), (wide, F32), ((2, FIELDS, 2, 8, CELL), F32),
        ((8, CELL), F32), ((4, 2 * CELL, CELL), BF16), ((2, 256, CELL), BF16), ((7, 8, CELL), F32),
    ]
    vmem, hbm = pl.BlockSpec(memory_space=pltpu.VMEM), pl.BlockSpec(memory_space=pltpu.HBM)

    def shards(coefficients, level_masks):
        held = pl.pallas_call(
            functools.partial(front, n_tile, n_lvl, inner, reach),
            out_shape=[pltpu.VMEM(shape, dtype) for shape, dtype in between],
            in_specs=[hbm, hbm],
            out_specs=[vmem] * len(between),
            scratch_shapes=[
                pltpu.VMEM(flat, F32), pltpu.SMEM((4, 1, 6), jnp.int32),
                pltpu.VMEM(wide, F32), pltpu.VMEM(wide, F32), pltpu.VMEM((7, 8, CELL), F32),
                pltpu.VMEM((2, 2, 16, CELL), F32), pltpu.VMEM((2, 2, 16, CELL), F32),
                pltpu.VMEM((2, 2, FIELDS, 8, CELL), F32), pltpu.VMEM((2, 2, FIELDS, 8, CELL), F32),
                pltpu.VMEM((2, 1, CELL), F32), pltpu.VMEM((2, most, 1, CELL), F32),
                dma((FIELDS,)), dma(()),
                dma((2, 2)), dma((2, 2)), dma((2, 2)), dma((2, 2)), dma((2,)), dma((2,)),
            ],
            compiler_params=pltpu.CompilerParams(
                collective_id=0, has_side_effects=True, vmem_limit_bytes=57 * 2**20
            ),
        )(coefficients, level_masks)
        result = jax.ShapeDtypeStruct((FIELDS, ROWS, CELL), F32)
        return pl.pallas_call(
            back,
            out_shape=(result, result),
            in_specs=[vmem] * len(between),
            out_specs=(hbm, hbm),
            scratch_shapes=[
                pltpu.VMEM(flat, F32), pltpu.VMEM(flat, F32), pltpu.VMEM(wide, F32),
                pltpu.VMEM(wide, F32), dma((2, FIELDS)),
            ],
            compiler_params=pltpu.CompilerParams(vmem_limit_bytes=24 * 2**20),
        )(*held)

    specs = P(None, "tile", "lvl")
    return jax.shard_map(
        shards, mesh=mesh, in_specs=(specs, P("tile", "lvl", None)), out_specs=(specs, specs),
        check_vma=False,
    )
```

time: 40.8 us -> 34.5 us (0.85)
  local copies, waits for them, and re-layouts: 4.11 us -> 0 us
  Pallas kernels: 35.8 us -> 33.8 us
    unnamed x6 -> x0, local copies, waits for them, and re-layouts: 4.11 us -> none
    pallas_call x1 -> x2, Pallas kernels: 35.8 us -> 33.8 us  [the longest x1 29.5 us: shards(): pl.pallas_call(functools.partial(front, n_tile, n_lvl, inner, reach), out...]
where the time goes in v2:
time: 34.5 us; the launch traced here: 34.4 us
  Pallas kernels  33.8 us (98%)
  between operations  0.64 us (2%)
    pallas_call x1, Pallas kernels, shards(): pl.pallas_call(functools.partial(front, n_tile, n_lvl, inner, reach), out...  29.5 us
    pallas_call x1, Pallas kernels, shards(): pl.pallas_call(back, out_shape=(result, result), in_specs=[vmem] * len(be...  4.3 us

profile of v2, /device:TPU:1, one launch (start us, length us, event | category | flops | bytes accessed | tf_op | source)
XLA Modules:
  0.0 34.4 jit_solution(3905891725106916178)
XLA Ops:
  0.6 29.5 %shard_map.41 = (f32[5,64,8,128]{3,2,1,0:T(8,128)S(1)}, f32[5,64,8,128]{3,2,1,0:T(8,128)S(1)}, f32[5,68,8,128]{3,2,1,0:T(8,128)S(1)}, f32[5,68,8,128]{3,2,1,0:T(...) custom-call(f32[5,512,128]{2,1,0:T(8,128)} %coef.1, ...), custom_call_target="tpu_custom_call" | custom-call | tf_op jit(solution)/shard_map/pallas_call | solution.py:423
  30.1 4.3 %shard_map.42 = (f32[5,512,128]{2,1,0:T(8,128)}, f32[5,512,128]{2,1,0:T(8,128)}) custom-call(f32[5,64,8,128]{3,2,1,0:T(8,128)S(1)} %get-tuple-element.11.start, f32[5,64,8,128]{3,2,1,0:T(8,128)S(1)} %get-tuple-element.12.half0, f32[5,68,8,128]{3,2,1,0:T(8,128)S(1)} %get-tuple-element.13.st, f32[5,68,8,128]{3,2,1,0:T(8,128)S(1)} %get-tuple-element.14.rr, ...), custom_call_target="tpu_custom_call" | custom-call | tf_op jit(solution)/shard_map/pallas_call | solution.py:442

commit v3 on v2

--- a/solution.py
+++ b/solution.py
@@ -13,6 +13,7 @@
 FIELDS = 5
 CELL = 128
 SEG = 64
+PITCH = 72
 ROWS = 512
 BASE_DENSITY = 1.0
 BASE_ENERGY = 2.5
@@ -153,7 +154,7 @@
 EXT = SEG + 4
 
 
-def flux_pass(state_at, fx, fy):
+def flux_pass(state_at, fx, fy, unroll=False):
     def chunk(c, _):
         rows = pl.ds(c * CHUNK, CHUNK)
         q = state_at(rows)
@@ -164,42 +165,41 @@
             fy[f, rows] = value
         return 0
 
-    lax.fori_loop(0, EXT // CHUNK, chunk, 0)
-
-
-def analysed(f, edge, fx, fy, wmat, hmask, even):
+    lax.fori_loop(0, EXT // CHUNK, chunk, 0, unroll=unroll)
+
+
+def analysed(f, edge, fx, fy, wmat, spread, even):
     g = fx[f]
     slope = 8.0 * (g[3:67] - g[1:65]) - (g[4:68] - g[0:64])
     xh, xl = halves(slope.reshape(ROWS, CELL))
     yh, yl = halves(fy[f, 2:66].reshape(ROWS, CELL))
-    weights = wmat[1]
-    out = dot(jnp.concatenate([xh, yh], 1), weights) + dot(jnp.concatenate([xl, yl], 1), weights)
-    extra = []
+    out = []
     for part in range(2):
         eh, el = halves(jnp.concatenate([edge[part], edge[part]], 0))
-        spread = hmask[part]
-        eh = jnp.concatenate([eh] * 16, 0) * spread
-        el = jnp.concatenate([el] * 16, 0) * spread
-        extra.append(dot(jnp.concatenate([eh, el], 1), wmat[2 + part]))
-    out = out + jnp.concatenate(extra, 0)
-    return row_analysis(out.reshape(SEG, 8, CELL), even)
-
-
-def build_weights(wmat, hmask):
+        mask = spread[part]
+        eh = jnp.concatenate([eh] * 16, 0) * mask
+        el = jnp.concatenate([el] * 16, 0) * mask
+        rows = slice(part * 256, part * 256 + 256)
+        terms = [xh[rows], yh[rows], xl[rows], yl[rows], eh, el]
+        out.append(dot(jnp.concatenate(terms, 1), wmat[1 + part]))
+    return row_analysis(jnp.concatenate(out, 0).reshape(SEG, 8, CELL), even)
+
+
+def build_weights(wmat, spread):
     synth = synthesis_t().astype(BF16)
     at = analysis_t().astype(BF16)
     k, i = iota((CELL, CELL), 0), iota((CELL, CELL), 1)
-    wmat[0, :CELL], wmat[0, CELL:] = synth, synth
-    wmat[1, :CELL] = at
-    wmat[1, CELL:] = dot(slope_matrix(k, i).astype(BF16), at).astype(BF16)
-    for part, offset in ((2, 2), (3, 0)):
+    wmat[0, :CELL], wmat[0, CELL:2 * CELL] = synth, synth
+    slope = dot(slope_matrix(k, i).astype(BF16), at).astype(BF16)
+    for part, offset in ((0, 2), (1, 0)):
         edge = slope_matrix(halo_point(jnp.bitwise_and(k + offset, 3)), i).astype(BF16)
         edge = dot(edge, at).astype(BF16)
-        wmat[part, :CELL], wmat[part, CELL:] = edge, edge
+        for number, block in enumerate((at, slope, at, slope, edge, edge)):
+            wmat[1 + part, number * CELL:(number + 1) * CELL] = block
     row, col = iota((32 * 8, CELL), 0), iota((32 * 8, CELL), 1)
     for part, offset in ((0, 2), (1, 0)):
         group = jnp.right_shift(jnp.bitwise_and(col + offset, 127), 2)
-        hmask[part] = jnp.where(group == jnp.right_shift(row, 3), 1.0, 0.0).astype(BF16)
+        spread[part] = jnp.where(group == jnp.right_shift(row, 3), 1.0, 0.0).astype(BF16)
 
 
 def build_keep(masks, mk, mkd, sub, lane):
@@ -222,7 +222,7 @@
 def front(
     n_tile, n_lvl, inner, reach,
     coef, masks,
-    start, half0, st, rr, cols, dts, wmat, hmask, mkd,
+    start, half0, st, rr, cols, dts, wmat, spread, mkd,
     cin, lvm, fx, fy, mk,
     row_snd, row_rcv, col_snd, col_rcv, mx_snd, mx_rcv,
     in_sem, mask_sem, row_ss, row_rs, col_ss, col_rs, mx_ss, mx_rs,
@@ -233,43 +233,42 @@
     t_right, t_left = lax.rem(tile + 1, n_tile), lax.rem(tile + n_tile - 1, n_tile)
     l_right, l_left = lax.rem(lvl + 1, n_lvl), lax.rem(lvl + n_lvl - 1, n_lvl)
 
-    load_masks = pltpu.make_async_copy(masks, lvm, mask_sem)
-    load_masks.start()
-    load = [
-        pltpu.make_async_copy(coef.at[f], cin.at[pl.ds(f * ROWS, ROWS)], in_sem.at[f])
-        for f in range(FIELDS)
+    def there(dz, dlow, dx):
+        to = lax.rem(z + dz, outer) * inner + lax.rem(low + dlow, inner)
+        return to, lax.rem(lvl + dx, n_lvl)
+
+    around = sorted(range(1, outer), key=lambda d: -min(d, outer - d))
+    plane = [(dlow, dx) for dx in range(n_lvl) for dlow in range(inner) if dlow or dx]
+    plane.sort(key=lambda d: -abs(min(d[0], inner - d[0])) // 2 - min(d[1], n_lvl - d[1]))
+    groups = [
+        [there(dz, 0, 0) for dz in around if min(dz, outer - dz) <= reach]
+        + [there(0, dlow, dx) for dlow, dx in plane],
+        [there(dz, 0, 0) for dz in around],
     ]
-    for copy in load:
-        copy.start()
-
-    def there(dz, dlow, dx):
-        to = lax.rem(z + outer + dz, outer) * inner + lax.rem(low + dlow, inner)
-        return to, lax.rem(lvl + dx, n_lvl)
-
-    spread = sorted(range(-reach, reach + 1), key=lambda d: -abs(d))
-    jumps = sorted({d % outer for d in (-reach, 0, reach)}, key=lambda d: d == 0)
-    spread = list(dict.fromkeys(d % outer for d in spread))
-    groups = [
-        [there(dz, 0, dx) for dz in spread for dx in range(n_lvl) if dz or dx],
-        [there(dz, dlow, 0) for dz in jumps for dlow in range(inner) if dz or dlow],
-    ]
-    partners = groups[0] + groups[1]
-    partners += [(t_right, lvl), (t_left, lvl), (tile, l_right), (tile, l_left)]
+    partners = groups[0] + [(t_right, lvl), (t_left, lvl), (tile, l_right), (tile, l_left)]
     barrier = pltpu.get_barrier_semaphore()
     for partner in partners:
         pl.semaphore_signal(barrier, inc=1, device_id=partner, device_id_type=MESH)
+
+    load_masks = pltpu.make_async_copy(masks, lvm, mask_sem)
+    load_masks.start()
+    for f in range(FIELDS):
+        for g in range(8):
+            pltpu.make_async_copy(
+                coef.at[f, pl.ds(g * SEG, SEG)], cin.at[pl.ds((f * 8 + g) * PITCH, SEG)],
+                in_sem.at[f]).start()
 
     sub, lane = iota((8, CELL), 0), iota((8, CELL), 1)
     even = jnp.bitwise_and(sub, 1) == 0
     upper = jnp.bitwise_and(lane, 3) >= 2
     coarse = jnp.bitwise_and(lane, 63) == 0
-    build_weights(wmat, hmask)
+    build_weights(wmat, spread)
     load_masks.wait()
     build_keep(lvm, mk, mkd, sub, lane)
 
     def synthesise(c):
         high, low_part = halves(c.reshape(ROWS, CELL))
-        out = dot(jnp.concatenate([high, low_part], 1), wmat[0])
+        out = dot(jnp.concatenate([high, low_part], 1), wmat[0, :2 * CELL])
         return row_synthesis(out.reshape(SEG, 8, CELL), even)
 
     def pack(stage, f, u):
@@ -321,8 +320,10 @@
             cols[stage, f, 1] = jnp.where(upper, from_right, from_left)
 
     for f in range(FIELDS):
-        load[f].wait()
-        parts = [cin[pl.ds(f * ROWS + p, 8, SEG), :] * mk[row_level(p)] for p in range(SEG)]
+        pltpu.make_async_copy(coef.at[f], cin.at[pl.ds(f * 8 * PITCH, ROWS)], in_sem.at[f]).wait()
+        parts = [
+            cin[pl.ds(f * 8 * PITCH + p, 8, PITCH), :] * mk[row_level(p)] for p in range(SEG)
+        ]
         parts = jnp.stack(parts, 0)
         start[f] = parts
         base = {0: BASE_DENSITY, 4: BASE_ENERGY}.get(f)
@@ -333,7 +334,6 @@
         if base:
             u = u + base
         st[f, 2:66] = u
-        pack(0, f, u)
 
     def fastest(c, top):
         rows = pl.ds(c * CHUNK + 2, CHUNK)
@@ -346,27 +346,31 @@
     pl.semaphore_wait(barrier, len(partners))
     first_round, second_round = rounds(0), rounds(1)
     edges = [edge_copies(0), edge_copies(1)]
-    for copy in first_round + edges[0]:
+    for copy in first_round:
+        copy.start()
+    for f in range(FIELDS):
+        pack(0, f, st[f, 2:66])
+    for copy in edges[0]:
         copy.start()
 
     for copy in edges[0]:
         copy.wait_recv()
+    top = take_top(0, top)
+    mx_snd[1] = top
+    for copy in second_round:
+        copy.start()
     take_edges(0, st)
     flux_pass(lambda rows: [st[f, rows] for f in range(FIELDS)], fx, fy)
     q = [cols[0, f] for f in range(FIELDS)]
-    edge_flux = y_flux(q, primitives(q))
-    for f in range(FIELDS):
-        d = analysed(f, edge_flux[f], fx, fy, wmat, hmask, even)
+    edge = y_flux(q, primitives(q))
+    for f in range(FIELDS):
+        d = analysed(f, edge[f], fx, fy, wmat, spread, even)
         half = jnp.stack([d[p] * mkd[row_level(p)] for p in range(SEG)], 0)
         half0[f] = half
         u = synthesise(half + half)
         rr[f, 2:66] = u
         pack(1, f, u)
     for copy in edges[1]:
-        copy.start()
-    top = take_top(0, top)
-    mx_snd[1] = top
-    for copy in second_round:
         copy.start()
     for copy in edges[1]:
         copy.wait_recv()
@@ -381,28 +385,30 @@
 
 
 def back(
-    start, half0, st, rr, cols, dts, wmat, hmask, mkd, adv, ten, oadv, oten, fx, fy, out_sem
+    start, half0, st, rr, cols, dts, wmat, spread, mkd, adv, ten, oadv, oten, fx, fy, out_sem
 ):
     even = jnp.bitwise_and(iota((8, CELL), 0), 1) == 0
     dt = dts[...]
-    flux_pass(lambda rows: [st[f, rows] + dt * rr[f, rows] for f in range(FIELDS)], fx, fy)
+    flux_pass(lambda rows: [st[f, rows] + dt * rr[f, rows] for f in range(FIELDS)], fx, fy, True)
     q = [cols[0, f] + dt * cols[1, f] for f in range(FIELDS)]
-    edge_flux = y_flux(q, primitives(q))
-    store = []
-    for f in range(FIELDS):
-        d = analysed(f, edge_flux[f], fx, fy, wmat, hmask, even)
+    edge = y_flux(q, primitives(q))
+    results = ((oadv, adv), (oten, ten))
+    for f in range(FIELDS):
+        d = analysed(f, edge[f], fx, fy, wmat, spread, even)
         for p in range(SEG):
             value = half0[f, p] + d[p] * mkd[row_level(p)]
-            rows = pl.ds(f * ROWS + p, 8, SEG)
+            rows = pl.ds(f * 8 * PITCH + p, 8, PITCH)
             oten[rows, :] = value
             oadv[rows, :] = start[f, p] + dt * value
-        for number, (source, target) in enumerate(((oadv, adv), (oten, ten))):
-            copy = pltpu.make_async_copy(
-                source.at[pl.ds(f * ROWS, ROWS)], target.at[f], out_sem.at[number, f])
-            copy.start()
-            store.append(copy)
-    for copy in store:
-        copy.wait()
+        for number, (source, target) in enumerate(results):
+            for g in range(8):
+                pltpu.make_async_copy(
+                    source.at[pl.ds((f * 8 + g) * PITCH, SEG)], target.at[f, pl.ds(g * SEG, SEG)],
+                    out_sem.at[number, f]).start()
+    for f in range(FIELDS):
+        for number, (source, target) in enumerate(results):
+            pltpu.make_async_copy(
+                source.at[pl.ds(f * 8 * PITCH, ROWS)], target.at[f], out_sem.at[number, f]).wait()
 
 
 def solution(mesh):
@@ -410,12 +416,13 @@
     inner = 8 if n_tile > 8 and n_tile % 8 == 0 else 2
     reach = -(-(n_tile // inner) // 4)
     block, wide = (FIELDS, SEG, 8, CELL), (FIELDS, EXT, 8, CELL)
-    flat = (FIELDS * ROWS, CELL)
-    most = max((2 * reach + 1) * n_lvl, 3 * inner)
+    flat = (FIELDS * 8 * PITCH, CELL)
+    most = max(inner * n_lvl + 2 * reach, n_tile // inner)
     dma = pltpu.SemaphoreType.DMA
     between = [
         (block, F32), (block, F32), (wide, F32), (wide, F32), ((2, FIELDS, 2, 8, CELL), F32),
-        ((8, CELL), F32), ((4, 2 * CELL, CELL), BF16), ((2, 256, CELL), BF16), ((7, 8, CELL), F32),
+        ((8, CELL), F32), ((3, 6 * CELL, CELL), BF16), ((2, 256, CELL), BF16),
+        ((7, 8, CELL), F32),
     ]
     vmem, hbm = pl.BlockSpec(memory_space=pltpu.VMEM), pl.BlockSpec(memory_space=pltpu.HBM)
 

time: 34.5 us -> 30.3 us (0.88)
  Pallas kernels: 33.8 us -> 29.5 us
    pallas_call x1, Pallas kernels: 29.5 us -> 26.9 us  [shards(): pl.pallas_call(functools.partial(front, n_tile, n_lvl, inner, reach), out...]
    pallas_call x1, Pallas kernels: 4.3 us -> 2.6 us  [shards(): pl.pallas_call(back, out_shape=(result, result), in_specs=[vmem] * len(be...]
where the time goes in v3:
time: 30.3 us; the launch traced here: 30.2 us
  Pallas kernels  29.5 us (97%)
  between operations  0.64 us (2%)
    pallas_call x1, Pallas kernels, shards(): pl.pallas_call(functools.partial(front, n_tile, n_lvl, inner, reach), out...  26.9 us
    pallas_call x1, Pallas kernels, shards(): pl.pallas_call(back, out_shape=(result, result), in_specs=[vmem] * len(be...  2.6 us

profile of v3, /device:TPU:1, one launch (start us, length us, event | category | flops | bytes accessed | tf_op | source)
XLA Modules:
  0.0 30.2 jit_solution(10248794195068041712)
XLA Ops:
  0.6 26.9 %shard_map.41 = (f32[5,64,8,128]{3,2,1,0:T(8,128)S(1)}, f32[5,64,8,128]{3,2,1,0:T(8,128)S(1)}, f32[5,68,8,128]{3,2,1,0:T(8,128)S(1)}, f32[5,68,8,128]{3,2,1,0:T(...) custom-call(f32[5,512,128]{2,1,0:T(8,128)} %coef.1, ...), custom_call_target="tpu_custom_call" | custom-call | tf_op jit(solution)/shard_map/pallas_call | solution.py:430
  27.6 2.6 %shard_map.42 = (f32[5,512,128]{2,1,0:T(8,128)}, f32[5,512,128]{2,1,0:T(8,128)}) custom-call(f32[5,64,8,128]{3,2,1,0:T(8,128)S(1)} %get-tuple-element.11.start, f32[5,64,8,128]{3,2,1,0:T(8,128)S(1)} %get-tuple-element.12.half0, f32[5,68,8,128]{3,2,1,0:T(8,128)S(1)} %get-tuple-element.13.st, f32[5,68,8,128]{3,2,1,0:T(8,128)S(1)} %get-tuple-element.14.rr, ...), custom_call_target="tpu_custom_call" | custom-call | tf_op jit(solution)/shard_map/pallas_call | solution.py:449

commit v4 on v3

--- a/solution.py
+++ b/solution.py
@@ -247,9 +247,6 @@
     ]
     partners = groups[0] + [(t_right, lvl), (t_left, lvl), (tile, l_right), (tile, l_left)]
     barrier = pltpu.get_barrier_semaphore()
-    for partner in partners:
-        pl.semaphore_signal(barrier, inc=1, device_id=partner, device_id_type=MESH)
-
     load_masks = pltpu.make_async_copy(masks, lvm, mask_sem)
     load_masks.start()
     for f in range(FIELDS):
@@ -257,6 +254,9 @@
             pltpu.make_async_copy(
                 coef.at[f, pl.ds(g * SEG, SEG)], cin.at[pl.ds((f * 8 + g) * PITCH, SEG)],
                 in_sem.at[f]).start()
+
+    for partner in partners:
+        pl.semaphore_signal(barrier, inc=1, device_id=partner, device_id_type=MESH)
 
     sub, lane = iota((8, CELL), 0), iota((8, CELL), 1)
     even = jnp.bitwise_and(sub, 1) == 0
@@ -340,7 +340,7 @@
         prim = primitives([st[f, rows] for f in range(FIELDS)])
         return jnp.maximum(top, jnp.max(speed(prim), 0))
 
-    top = lax.fori_loop(0, SEG // CHUNK, fastest, jnp.zeros((8, CELL), F32))
+    top = lax.fori_loop(0, SEG // CHUNK, fastest, jnp.zeros((8, CELL), F32), unroll=True)
     top = jnp.max(top, 0, keepdims=True)
     mx_snd[0] = top
     pl.semaphore_wait(barrier, len(partners))

time: 30.3 us -> 29.5 us (0.974)
  Pallas kernels: 29.5 us -> 28.7 us
    pallas_call x1, Pallas kernels: 26.9 us -> 26.1 us  [shards(): pl.pallas_call(functools.partial(front, n_tile, n_lvl, inner, reach), out...]
where the time goes in v4:
time: 29.5 us; the launch traced here: 29.3 us
  Pallas kernels  28.7 us (97%)
  between operations  0.64 us (2%)
    pallas_call x1, Pallas kernels, shards(): pl.pallas_call(functools.partial(front, n_tile, n_lvl, inner, reach), out...  26.1 us
    pallas_call x1, Pallas kernels, shards(): pl.pallas_call(back, out_shape=(result, result), in_specs=[vmem] * len(be...  2.61 us

profile of v4, /device:TPU:1, one launch (start us, length us, event | category | flops | bytes accessed | tf_op | source)
XLA Modules:
  0.0 29.3 jit_solution(13884468347284920763)
XLA Ops:
  0.6 26.1 %shard_map.41 = (f32[5,64,8,128]{3,2,1,0:T(8,128)S(1)}, f32[5,64,8,128]{3,2,1,0:T(8,128)S(1)}, f32[5,68,8,128]{3,2,1,0:T(8,128)S(1)}, f32[5,68,8,128]{3,2,1,0:T(...) custom-call(f32[5,512,128]{2,1,0:T(8,128)} %coef.1, ...), custom_call_target="tpu_custom_call" | custom-call | tf_op jit(solution)/shard_map/pallas_call | solution.py:430
  26.7 2.6 %shard_map.42 = (f32[5,512,128]{2,1,0:T(8,128)}, f32[5,512,128]{2,1,0:T(8,128)}) custom-call(f32[5,64,8,128]{3,2,1,0:T(8,128)S(1)} %get-tuple-element.11.start, f32[5,64,8,128]{3,2,1,0:T(8,128)S(1)} %get-tuple-element.12.half0, f32[5,68,8,128]{3,2,1,0:T(8,128)S(1)} %get-tuple-element.13.st, f32[5,68,8,128]{3,2,1,0:T(8,128)S(1)} %get-tuple-element.14.rr, ...), custom_call_target="tpu_custom_call" | custom-call | tf_op jit(solution)/shard_map/pallas_call | solution.py:449

commit v5 on v4

--- a/solution.py
+++ b/solution.py
@@ -321,6 +321,7 @@
 
     for f in range(FIELDS):
         pltpu.make_async_copy(coef.at[f], cin.at[pl.ds(f * 8 * PITCH, ROWS)], in_sem.at[f]).wait()
+    for f in range(FIELDS):
         parts = [
             cin[pl.ds(f * 8 * PITCH + p, 8, PITCH), :] * mk[row_level(p)] for p in range(SEG)
         ]
@@ -375,13 +376,11 @@
     for copy in edges[1]:
         copy.wait_recv()
     take_edges(1, rr)
-    for copy in edges[0] + edges[1] + first_round:
+    for copy in edges[0] + edges[1] + first_round + second_round:
         copy.wait_send()
     top = take_top(1, top)
     top = jnp.max(top, 1, keepdims=True)
     dts[...] = 0.5 * SPACING / jnp.broadcast_to(top, (8, CELL))
-    for copy in second_round:
-        copy.wait_send()
 
 
 def back(

time: 29.5 us -> 29.5 us (level)
  no operation moved by 1% of the time
where the time goes in v5:
time: 29.5 us; the launch traced here: 29.3 us
  Pallas kernels  28.6 us (97%)
  between operations  0.64 us (2%)
    pallas_call x1, Pallas kernels, shards(): pl.pallas_call(functools.partial(front, n_tile, n_lvl, inner, reach), out...  26 us
    pallas_call x1, Pallas kernels, shards(): pl.pallas_call(back, out_shape=(result, result), in_specs=[vmem] * len(be...  2.61 us

profile of v5, /device:TPU:1, one launch (start us, length us, event | category | flops | bytes accessed | tf_op | source)
XLA Modules:
  0.0 29.3 jit_solution(11789836914809014998)
XLA Ops:
  0.6 26.0 %shard_map.41 = (f32[5,64,8,128]{3,2,1,0:T(8,128)S(1)}, f32[5,64,8,128]{3,2,1,0:T(8,128)S(1)}, f32[5,68,8,128]{3,2,1,0:T(8,128)S(1)}, f32[5,68,8,128]{3,2,1,0:T(...) custom-call(f32[5,512,128]{2,1,0:T(8,128)} %coef.1, ...), custom_call_target="tpu_custom_call" | custom-call | tf_op jit(solution)/shard_map/pallas_call | solution.py:429
  26.7 2.6 %shard_map.42 = (f32[5,512,128]{2,1,0:T(8,128)}, f32[5,512,128]{2,1,0:T(8,128)}) custom-call(f32[5,64,8,128]{3,2,1,0:T(8,128)S(1)} %get-tuple-element.11.start, f32[5,64,8,128]{3,2,1,0:T(8,128)S(1)} %get-tuple-element.12.half0, f32[5,68,8,128]{3,2,1,0:T(8,128)S(1)} %get-tuple-element.13.st, f32[5,68,8,128]{3,2,1,0:T(8,128)S(1)} %get-tuple-element.14.rr, ...), custom_call_target="tpu_custom_call" | custom-call | tf_op jit(solution)/shard_map/pallas_call | solution.py:448

commit v6 on v3

--- a/solution.py
+++ b/solution.py
@@ -321,6 +321,7 @@
 
     for f in range(FIELDS):
         pltpu.make_async_copy(coef.at[f], cin.at[pl.ds(f * 8 * PITCH, ROWS)], in_sem.at[f]).wait()
+    for f in range(FIELDS):
         parts = [
             cin[pl.ds(f * 8 * PITCH + p, 8, PITCH), :] * mk[row_level(p)] for p in range(SEG)
         ]
@@ -340,7 +341,7 @@
         prim = primitives([st[f, rows] for f in range(FIELDS)])
         return jnp.maximum(top, jnp.max(speed(prim), 0))
 
-    top = lax.fori_loop(0, SEG // CHUNK, fastest, jnp.zeros((8, CELL), F32))
+    top = lax.fori_loop(0, SEG // CHUNK, fastest, jnp.zeros((8, CELL), F32), unroll=True)
     top = jnp.max(top, 0, keepdims=True)
     mx_snd[0] = top
     pl.semaphore_wait(barrier, len(partners))

time: 30.3 us -> 29.5 us (0.974)
  Pallas kernels: 29.5 us -> 28.7 us
    pallas_call x1, Pallas kernels: 26.9 us -> 26.1 us  [shards(): pl.pallas_call(functools.partial(front, n_tile, n_lvl, inner, reach), out...]
where the time goes in v6:
time: 29.5 us; the launch traced here: 29.3 us
  Pallas kernels  28.7 us (97%)
  between operations  0.64 us (2%)
    pallas_call x1, Pallas kernels, shards(): pl.pallas_call(functools.partial(front, n_tile, n_lvl, inner, reach), out...  26.1 us
    pallas_call x1, Pallas kernels, shards(): pl.pallas_call(back, out_shape=(result, result), in_specs=[vmem] * len(be...  2.61 us

profile of v6, /device:TPU:1, one launch (start us, length us, event | category | flops | bytes accessed | tf_op | source)
XLA Modules:
  0.0 29.3 jit_solution(9419117592910687935)
XLA Ops:
  0.6 26.1 %shard_map.41 = (f32[5,64,8,128]{3,2,1,0:T(8,128)S(1)}, f32[5,64,8,128]{3,2,1,0:T(8,128)S(1)}, f32[5,68,8,128]{3,2,1,0:T(8,128)S(1)}, f32[5,68,8,128]{3,2,1,0:T(...) custom-call(f32[5,512,128]{2,1,0:T(8,128)} %coef.1, ...), custom_call_target="tpu_custom_call" | custom-call | tf_op jit(solution)/shard_map/pallas_call | solution.py:431
  26.7 2.6 %shard_map.42 = (f32[5,512,128]{2,1,0:T(8,128)}, f32[5,512,128]{2,1,0:T(8,128)}) custom-call(f32[5,64,8,128]{3,2,1,0:T(8,128)S(1)} %get-tuple-element.11.start, f32[5,64,8,128]{3,2,1,0:T(8,128)S(1)} %get-tuple-element.12.half0, f32[5,68,8,128]{3,2,1,0:T(8,128)S(1)} %get-tuple-element.13.st, f32[5,68,8,128]{3,2,1,0:T(8,128)S(1)} %get-tuple-element.14.rr, ...), custom_call_target="tpu_custom_call" | custom-call | tf_op jit(solution)/shard_map/pallas_call | solution.py:450
